TPU v7x, 32 devices: a whole 2x2x4 slice. The times are simulated.
32 devices in a mesh: parts: 2 (over y), feat: 4 (over z), store: 4 (over x, core).
Axes of the slice: x: 2, y: 2, z: 4, core: 2. Of those that a mesh axis runs over, the one named last changes fastest.
Arguments:
- queries: bfloat16 [8192, 65536], P(('parts', 'store'), 'feat'), parts along dimension 0, may hold values from -6 to 6
- store_rows: bfloat16 [4096, 65536], P(('parts', 'store'), 'feat'), parts along dimension 0, may hold values from -0.03125 to 0.03125
- feature_scale: float32 [65536], P('feat'), may hold values from 0.1 to 10
Outputs:
- scores: float32 [2048, 8192], P('feat', ('parts', 'store')), parts along dimension 1
There are 2 independent parts, one for each index of `parts`. A program takes and returns all parts, laid end to end along the dimension named above; an argument that names none is the same for every part. Nothing has to cross between parts.
All inputs are finite; a program needn't handle non-finite values.
Results may differ from a plain program's by a relative error of at most 0.0029.
Values may be sent and summed in bfloat16 or wider, within the bound.
A program may use at most 256 MiB of HBM per device.

v0:
```python
import jax
import jax.numpy as jnp
from jax import lax
from jax.sharding import PartitionSpec as P


def passed_along(block, axis, distance):
    devices = range(lax.axis_size(axis))
    route = [((i - distance) % len(devices), i) for i in devices]
    return lax.ppermute(block, axis, route)


def local(queries, store_rows, feature_scale):
    scaled = (queries.astype(jnp.float32) * feature_scale[None, :]).astype(jnp.bfloat16)
    window_len = store_rows.shape[0]
    members = lax.axis_size("store")
    window_all = window_len * members
    contract = (((1,), (1,)), ((), ()))
    partials = jnp.zeros((window_all, scaled.shape[0]), jnp.float32)
    current = store_rows
    position = lax.axis_index("store")
    for turn_index in range(members):
        if turn_index > 0:
            current = passed_along(current, "store", 1)
        anchor = (position - turn_index) % members
        tile_scores = lax.dot_general(current, scaled, contract, preferred_element_type=jnp.float32)
        partials = lax.dynamic_update_slice_in_dim(partials, tile_scores, anchor * window_len, 0)
    summed = lax.psum(partials, "feat")
    share_len = window_all // lax.axis_size("feat")
    return lax.dynamic_slice_in_dim(summed, lax.axis_index("feat") * share_len, share_len, 0)


def solution(mesh):
    return jax.shard_map(
        local,
        mesh=mesh,
        in_specs=(P(("parts", "store"), "feat"), P(("parts", "store"), "feat"), P("feat")),
        out_specs=P("feat", ("parts", "store")),
        check_vma=False,
    )
```

profile of v0, /device:TPU:14, one launch (start us, length us, event | category | flops | bytes accessed | tf_op | source)
XLA Modules:
  0.0 890.4 jit_solution(12176312721336461564)
XLA Ops:
  6.5 0.0 all-reduce.2.cloned.1.call-start
  6.5 0.0 collective-permute-start
  6.5 183.0 %collective-permute-done = bf16[512,16384]{1,0:T(8,128)(2,1)S(1)} collective-permute-done((bf16[512,16384]{1,0:T(8,128)(2,1)}, bf16[512,16384]{1,0:T(8,128)(2,1)S(1)}, u32[]{:S(2)}, u32[]{:S(2)}) %collective-permute-start) | collective-permute-done | bytes 16777248 | tf_op jit(solution)/shard_map/ppermute | solution.py:10
  189.5 0.0 copy-start
  189.5 5.7 copy-done
  195.2 0.0 collective-permute-start.1
  195.2 182.9 %collective-permute-done.1 = bf16[512,16384]{1,0:T(8,128)(2,1)} collective-permute-done((bf16[512,16384]{1,0:T(8,128)(2,1)S(1)}, bf16[512,16384]{1,0:T(8,128)(2,1)}, u32[]{:S(2)}, u32[]{:S(2)}) %collective-permute-start.1) | collective-permute-done | bytes 16777248 | tf_op jit(solution)/shard_map/ppermute | solution.py:10
  378.1 0.0 collective-permute-start.2
  378.1 25.7 %fusion.4 = f32[512,1024]{0,1:T(8,128)} fusion(bf16[512,16384]{1,0:T(8,128)(2,1)} %param.4, bf16[1024,16384]{1,0:T(8,128)(2,1)} %param.3, f32[16384]{0:T(1024)} %param.5), kind=kOutput, calls=%fused_computation.5 | convolution fusion | flops 17230200832 | bytes 52494336 | tf_op jit(solution)/shard_map/dot_general | solution.py:26
  403.8 0.0 copy-start.1
  403.8 2.0 copy.4
  405.7 4.3 broadcast_in_dim.4
  410.0 1.4 constant_dynamic-update-slice_fusion.3
  411.5 0.0 copy-done.1
  411.5 25.7 %fusion.5 = f32[512,1024]{0,1:T(8,128)} fusion(bf16[512,16384]{1,0:T(8,128)(2,1)} %copy-done, bf16[1024,16384]{1,0:T(8,128)(2,1)} %param.3, f32[16384]{0:T(1024)S(1)} %copy-done.1), kind=kOutput, calls=%fused_computation.6 | convolution fusion | flops 17230200832 | bytes 52494336 | tf_op jit(solution)/shard_map/dot_general | solution.py:26
  437.1 2.1 copy.5
  439.2 1.5 constant_dynamic-update-slice_fusion.2
  440.8 25.7 %fusion.6 = f32[512,1024]{0,1:T(8,128)} fusion(bf16[512,16384]{1,0:T(8,128)(2,1)} %collective-permute-done.1, bf16[1024,16384]{1,0:T(8,128)(2,1)} %param.3, f32[16384]{0:T(1024)S(1)} %copy-done.1), kind=kOutput, calls=%fused_computation.7 | convolution fusion | flops 17230200832 | bytes 52494336 | tf_op jit(solution)/shard_map/dot_general | solution.py:26
  466.4 1.9 copy.6
  468.3 1.5 constant_dynamic-update-slice_fusion.1
  469.8 91.3 %collective-permute-done.2 = bf16[512,16384]{1,0:T(8,128)(2,1)} collective-permute-done((bf16[512,16384]{1,0:T(8,128)(2,1)}, bf16[512,16384]{1,0:T(8,128)(2,1)}, u32[]{:S(2)}, u32[]{:S(2)}) %collective-permute-start.2) | collective-permute-done | bytes 16777248 | tf_op jit(solution)/shard_map/ppermute | solution.py:10
  561.1 25.7 %fusion.7 = f32[512,1024]{0,1:T(8,128)} fusion(bf16[512,16384]{1,0:T(8,128)(2,1)} %collective-permute-done.2, bf16[1024,16384]{1,0:T(8,128)(2,1)} %param.3, f32[16384]{0:T(1024)S(1)} %copy-done.1), kind=kOutput, calls=%fused_computation.8 | convolution fusion | flops 17230200832 | bytes 52494336 | tf_op jit(solution)/shard_map/dot_general | solution.py:26
  586.8 1.9 copy.7
  588.7 1.5 constant_dynamic-update-slice_fusion
  590.2 0.0 all-reduce.2.cloned.1.call-update
  590.2 290.1 %all-reduce.2.cloned.1.call-done = f32[2048,1024]{1,0:T(8,128)} async-done(((f32[2048,1024]{1,0:T(8,128)}), f32[2048,1024]{1,0:T(8,128)}) %all-reduce.2.cloned.1.call-update) | async-done | bytes 8388624 | tf_op jit(solution)/shard_map/psum | solution.py:28
  880.4 3.2 constant_dynamic-slice_fusion
Async XLA Ops:
  6.5 873.8 %all-reduce.2.cloned.1.call-start = ((), (), s32[]{:S(2)}) async-start(), calls=%async_computation | async-start | bytes 16777216 | tf_op jit(solution)/shard_map/psum | solution.py:28
  6.5 183.0 %collective-permute-start = (bf16[512,16384]{1,0:T(8,128)(2,1)}, bf16[512,16384]{1,0:T(8,128)(2,1)S(1)}, u32[]{:S(2)}, u32[]{:S(2)}) collective-permute-start(bf16[512,16384]{1,0:T(8,128)(2,1)} %param.4), channel_id=1, source_target_pairs={{3,0},{0,1},{1,2},{2,3},{7,4},{4,5},{5,6},{6,7},{11,8},{8,9},{9,10... | collective-permute-start | bytes 50331656 | tf_op jit(solution)/shard_map/ppermute | solution.py:10
  189.5 5.7 copy-start
  195.2 182.9 %collective-permute-start.1 = (bf16[512,16384]{1,0:T(8,128)(2,1)S(1)}, bf16[512,16384]{1,0:T(8,128)(2,1)}, u32[]{:S(2)}, u32[]{:S(2)}) collective-permute-start(bf16[512,16384]{1,0:T(8,128)(2,1)S(1)} %collective-permute-done), channel_id=1, source_target_pairs={{3,0},{0,1},{1,2},{2,3},{7,4},{4,5},{5,6},{6,7},{11,8},{8,9},{9,10... | collective-permute-start | bytes 50331656 | tf_op jit(solution)/shard_map/ppermute | solution.py:10
  378.1 183.1 %collective-permute-start.2 = (bf16[512,16384]{1,0:T(8,128)(2,1)}, bf16[512,16384]{1,0:T(8,128)(2,1)}, u32[]{:S(2)}, u32[]{:S(2)}) collective-permute-start(bf16[512,16384]{1,0:T(8,128)(2,1)} %collective-permute-done.1), channel_id=1, source_target_pairs={{3,0},{0,1},{1,2},{2,3},{7,4},{4,5},{5,6},{6,7},{11,8},{8,9},{9,10... | collective-permute-start | bytes 50331656 | tf_op jit(solution)/shard_map/ppermute | solution.py:10
  403.8 7.7 copy-start.1
Sparse Core Ops, SparseCore 0:
  590.3 289.9 all-reduce.1
where the time goes:
time: 894 us; the launch traced here: 890 us
  waiting for transfers between devices  747 us (84%)
  matrix products  103 us (12%)
  local copies, waits for them, and re-layouts  26.9 us (3%)
  between operations  13.5 us (2%)
    ppermute x3, waiting for transfers between devices, passed_along(): return lax.ppermute(block, axis, route)  457 us
    psum x1, waiting for transfers between devices, local(): summed = lax.psum(partials, 'feat')  290 us
    dot_general x4, matrix products, local(): lax.dot_general(current, scaled, contract, preferred_element_type=jnp.flo...  103 us
  transfers between devices with their start and end apart: 4, of which 4 were waited for; matrix products, arithmetic and copies ran while one was open for 10% of the time, Pallas kernels for 0%

commit v1 on v0

v1 whole, which is shorter than its diff:
```python
import functools

import jax
import jax.numpy as jnp
from jax import lax
from jax.experimental import pallas as pl
from jax.experimental.pallas import tpu as pltpu
from jax.sharding import PartitionSpec as P

MESH = pl.DeviceIdType.MESH
EARLY_ROWS = 128
LATE_ROWS = 32
PIECE = 4096
AHEAD = 4
BURST = 16
SLOTS = 4
NT = 256


def kernel(n_feat, cfg, queries, store, scale, out, got, q, stage, acc_e, acc_l, recv,
           q_sem, load_sem, sib_send, sib_recv, x_send, x_recv, relay_send, relay_recv,
           red_send_e, red_recv_e, red_send_l, red_recv_l):
    W, K, NQ, share, Re, Rl, Kp, QR = cfg
    nk = K // Kp
    n_early, n_late = W // Re, W // Rl
    pieces_e, pieces = n_early * nk, n_late * nk
    s = lax.axis_index("store")
    me = lax.axis_index("feat")
    sib = s + 1 - 2 * lax.rem(s, 2)
    partner = lax.rem(s + 2, 4)
    far = lax.rem(sib + 2, 4)

    def q_copy(i):
        rows = pl.ds(pl.multiple_of(i * QR, QR), QR)
        return pltpu.make_async_copy(queries.at[rows], q.at[rows], q_sem.at[i])

    def sib_copy(c):
        rows = pl.ds(pl.multiple_of(c * Re, Re), Re)
        return pltpu.make_async_remote_copy(
            store.at[rows], got.at[0, rows], sib_send.at[c], sib_recv.at[c],
            device_id={"store": sib}, device_id_type=MESH)

    def where(p):
        return (pl.ds(pl.multiple_of((p // nk) * Rl, Rl), Rl),
                pl.ds(pl.multiple_of((p % nk) * Kp, Kp), Kp))

    def x_copy(p):
        rows, cols = where(p)
        return pltpu.make_async_remote_copy(
            store.at[rows, cols], got.at[1, rows, cols], x_send.at[p], x_recv.at[p],
            device_id={"store": partner}, device_id_type=MESH)

    def relay_copy(p):
        rows, cols = where(p)
        return pltpu.make_async_remote_copy(
            got.at[1, rows, cols], got.at[2, rows, cols], relay_send.at[p], relay_recv.at[p],
            device_id={"store": sib}, device_id_type=MESH)

    def load_late(p, half):
        rows, cols = where(p)
        slot = lax.rem(p, 2)
        return pltpu.make_async_copy(
            got.at[1 + half, rows, cols], stage.at[slot, pl.ds(half * Rl, Rl)],
            load_sem.at[slot, half])

    def load_early(p, half):
        rows = pl.ds(pl.multiple_of((p // nk) * Re, Re), Re)
        cols = pl.ds(pl.multiple_of((p % nk) * Kp, Kp), Kp)
        slot = lax.rem(p, 2)
        src = store.at[rows, cols] if half == 0 else got.at[0, rows, cols]
        return pltpu.make_async_copy(
            src, stage.at[slot, pl.ds(half * Re, Re)], load_sem.at[slot, half])

    barrier = pltpu.get_barrier_semaphore()
    for target in (sib, partner):
        pl.semaphore_signal(barrier, inc=1, device_id={"store": target}, device_id_type=MESH)

    @pl.loop(1, n_feat)
    def _(d):
        pl.semaphore_signal(barrier, inc=1, device_id={"feat": lax.rem(me + d, n_feat)},
                            device_id_type=MESH)

    @pl.loop(0, NQ // QR)
    def _(i):
        q_copy(i).start()

    load_early(0, 0).start()
    pl.semaphore_wait(barrier, n_feat + 1)

    burst = min(BURST, pieces)

    @pl.loop(0, burst)
    def _(p):
        x_copy(p).start()

    @pl.loop(0, n_early)
    def _(c):
        sib_copy(c).start()

    @pl.loop(0, NQ // QR)
    def _(i):
        q_copy(i).wait()

        @pl.loop(0, QR // 16)
        def _(j):
            rows = pl.ds(pl.multiple_of(i * QR + j * 16, 16), 16)
            for k0 in range(0, K, 2048):
                part = q[rows, k0:k0 + 2048].astype(jnp.float32) * scale[:, k0:k0 + 2048]
                q[rows, k0:k0 + 2048] = part.astype(jnp.bfloat16)

    def multiply(acc, p, R):
        slot = lax.rem(p, 2)
        k = lax.rem(p, nk)
        cols = pl.ds(pl.multiple_of(k * Kp, Kp), Kp)

        @pl.when(k == 0)
        def _():
            acc[...] = jnp.zeros(acc.shape, jnp.float32)

        for n0 in range(0, NQ, NT):
            acc[:, n0:n0 + NT] += lax.dot_general(
                stage[slot, :2 * R], q[n0:n0 + NT, cols], (((1,), (1,)), ((), ())),
                preferred_element_type=jnp.float32)

    def half_at(block, c, R):
        row = block * W + c * R
        return row // share, lax.rem(row, share)

    def send(acc, block, c, R, half, send_sem, recv_sem):
        t, off = half_at(block, c, R)
        return t, off, pltpu.make_async_remote_copy(
            acc.at[pl.ds(half * R, R)], recv.at[me, pl.ds(pl.multiple_of(off, R), R)],
            send_sem, recv_sem.at[me, off // R],
            device_id={"feat": t}, device_id_type=MESH)

    def hand_on(acc, blocks, c, R, send_sems, recv_sem):
        for half in range(2):
            t, off, copy = send(acc, blocks[half], c, R, half, send_sems.at[half], recv_sem)

            @pl.when(t == me)
            def _():
                recv[me, pl.ds(pl.multiple_of(off, R), R)] = acc[half * R:(half + 1) * R]

            @pl.when(t != me)
            def _():
                copy.start()

    def wait_sent(acc, blocks, c, R, send_sems, recv_sem):
        for half in range(2):
            t, off, copy = send(acc, blocks[half], c, R, half, send_sems.at[half], recv_sem)

            @pl.when(t != me)
            def _():
                copy.wait_send()

    def collect(blocks, c, R, recv_sem):
        for half in range(2):
            t, off = half_at(blocks[half], c, R)

            @pl.when(t == me)
            def _():
                rows = pl.ds(pl.multiple_of(off, R), R)

                @pl.loop(1, n_feat)
                def _(d):
                    f = lax.rem(me + d, n_feat)
                    pltpu.make_async_copy(
                        recv.at[f, rows], recv.at[f, rows], recv_sem.at[f, off // R]).wait()

                total = recv[0, rows]
                for f in range(1, n_feat):
                    total = total + recv[f, rows]
                out[rows] = total

    early, late = (s, sib), (partner, far)

    sib_copy(0).wait_recv()
    load_early(0, 1).start()

    @pl.loop(0, pieces_e)
    def _(p):
        @pl.when(p + 1 < pieces_e)
        def _():
            load_early(p + 1, 0).start()

            @pl.when(lax.rem(p + 1, nk) == 0)
            def _():
                sib_copy((p + 1) // nk).wait_recv()

            load_early(p + 1, 1).start()

        for half in range(2):
            load_early(p, half).wait()
        c = p // nk
        multiply(acc_e.at[c], p, Re)

        @pl.when(lax.rem(p, nk) == nk - 1)
        def _():
            hand_on(acc_e.at[c], early, c, Re, red_send_e.at[c], red_recv_e)

    def front(p):
        x_copy(p).wait_recv()
        relay_copy(p).start()
        load_late(p, 0).start()
        x_copy(p).wait_send()

        @pl.when((p + AHEAD >= burst) & (p + AHEAD < pieces))
        def _():
            x_copy(p + AHEAD).start()

    def mid(p):
        relay_copy(p).wait_recv()
        load_late(p, 1).start()

    front(0)
    mid(0)

    @pl.loop(0, pieces)
    def _(p):
        c = p // nk
        k = lax.rem(p, nk)
        slot = lax.rem(c, SLOTS)

        @pl.when(p + 1 < pieces)
        def _():
            front(p + 1)

        @pl.when((k == 0) & (c >= SLOTS))
        def _():
            wait_sent(acc_l.at[slot], late, c - SLOTS, Rl, red_send_l.at[slot], red_recv_l)

        for half in range(2):
            load_late(p, half).wait()
        multiply(acc_l.at[slot], p, Rl)

        @pl.when(k == nk - 1)
        def _():
            hand_on(acc_l.at[slot], late, c, Rl, red_send_l.at[slot], red_recv_l)

        @pl.when(p + 1 < pieces)
        def _():
            mid(p + 1)

        @pl.when((k == nk - 1) & (c >= 2))
        def _():
            collect(late, c - 2, Rl, red_recv_l)

        @pl.when((k == nk - 1) & (c == (3 * n_late) // 4))
        def _():
            @pl.loop(0, n_early)
            def _(e):
                collect(early, e, Re, red_recv_e)

    for c in range(max(n_late - 2, 0), n_late):
        collect(late, c, Rl, red_recv_l)

    @pl.loop(0, n_early)
    def _(c):
        sib_copy(c).wait_send()
        wait_sent(acc_e.at[c], early, c, Re, red_send_e.at[c], red_recv_e)

    @pl.loop(0, pieces)
    def _(p):
        relay_copy(p).wait_send()

    for c in range(max(n_late - SLOTS, 0), n_late):
        wait_sent(acc_l.at[c % SLOTS], late, c, Rl, red_send_l.at[c % SLOTS], red_recv_l)


def solution(mesh):
    n_feat = mesh.shape["feat"]
    members = mesh.shape["store"]
    assert members == 4

    def local(queries, store_rows, feature_scale):
        NQ, K = queries.shape
        W = store_rows.shape[0]
        share = W * members // n_feat
        Re, Rl = min(EARLY_ROWS, share, W), min(LATE_ROWS, share, W)
        Kp = min(PIECE, K)
        QR = min(128, NQ)
        nk, n_early, n_late = K // Kp, W // Re, W // Rl
        pieces = n_late * nk
        any_space = pl.BlockSpec(memory_space=pl.ANY)
        vmem = pl.BlockSpec(memory_space=pltpu.VMEM)
        dma = pltpu.SemaphoreType.DMA
        result, _ = pl.pallas_call(
            functools.partial(kernel, n_feat, (W, K, NQ, share, Re, Rl, Kp, QR)),
            out_shape=(jax.ShapeDtypeStruct((share, NQ), jnp.float32),
                       jax.ShapeDtypeStruct((3, W, K), jnp.bfloat16)),
            in_specs=[any_space, any_space, vmem],
            out_specs=(vmem, any_space),
            scratch_shapes=[
                pltpu.VMEM((NQ, K), jnp.bfloat16),
                pltpu.VMEM((2, 2 * Re, Kp), jnp.bfloat16),
                pltpu.VMEM((n_early, 2 * Re, NQ), jnp.float32),
                pltpu.VMEM((SLOTS, 2 * Rl, NQ), jnp.float32),
                pltpu.VMEM((n_feat, share, NQ), jnp.float32),
                dma((NQ // QR,)), dma((2, 2)),
                dma((n_early,)), dma((n_early,)),
                dma((pieces,)), dma((pieces,)), dma((pieces,)), dma((pieces,)),
                dma((n_early, 2)), dma((n_feat, share // Re)),
                dma((SLOTS, 2)), dma((n_feat, share // Rl)),
            ],
            compiler_params=pltpu.CompilerParams(
                collective_id=0, has_side_effects=True, vmem_limit_bytes=58 * 2**20),
            cost_estimate=pl.CostEstimate(
                flops=2 * W * members * NQ * K, bytes_accessed=2 * K * (NQ + 7 * W),
                transcendentals=0),
        )(queries, store_rows, feature_scale.reshape(1, K))
        return result

    return jax.shard_map(
        local,
        mesh=mesh,
        in_specs=(P(("parts", "store"), "feat"), P(("parts", "store"), "feat"), P("feat")),
        out_specs=P("feat", ("parts", "store")),
        check_vma=False,
    )
```

time: 894 us -> 407 us (0.46)
  waiting for transfers between devices: 747 us -> 0 us
  Pallas kernels: 0 us -> 402 us
  matrix products: 103 us -> 0 us
  local copies, waits for them, and re-layouts: 26.9 us -> 3.16 us
  between operations: 13.5 us -> 0.01 us
    ppermute x3 -> x0, waiting for transfers between devices: 457 us -> none  [passed_along(): return lax.ppermute(block, axis, route)]
    pallas_call x0 -> x1, Pallas kernels: none -> 402 us  [local(): pl.pallas_call(functools.partial(kernel, n_feat, (W, K, NQ, share, Re, Rl...]
    psum x1 -> x0, waiting for transfers between devices: 290 us -> none  [local(): summed = lax.psum(partials, 'feat')]
    dot_general x4 -> x0, matrix products: 103 us -> none  [local(): lax.dot_general(current, scaled, contract, preferred_element_type=jnp.flo...]
  transfers between devices with their start and end apart: 4 -> 0, of which waited for: 4 -> 0; matrix products, arithmetic and copies ran while one was open for 10% -> 0% of each run, Pallas kernels for 0% -> 0%
where the time goes in v1:
time: 407 us; the launch traced here: 406 us
  Pallas kernels  402 us (99%)
    pallas_call x1, Pallas kernels, local(): pl.pallas_call(functools.partial(kernel, n_feat, (W, K, NQ, share, Re, Rl...  402 us

profile of v1, /device:TPU:14, one launch (start us, length us, event | category | flops | bytes accessed | tf_op | source)
XLA Modules:
  0.0 405.5 jit_solution(16510112099876533628)
XLA Ops:
  0.0 402.3 %shard_map.37 = (f32[512,1024]{1,0:T(8,128)}, bf16[3,512,16384]{2,1,0:T(8,128)(2,1)}) custom-call(bf16[1024,16384]{1,0:T(8,128)(2,1)} %queries.1, bf16[512,16384]{1,0:T(8,128)(2,1)} %store.1, f32[1,16384]{1,0:T(1,128)} %bitcast.1), custom_call_target="tpu_custom_call" | custom-call | flops 68719476736 | bytes 150994944 | tf_op jit(solution)/shard_map/pallas_call | solution.py:287
  402.3 3.2 copy.5

commit v2 on v1

--- a/solution.py
+++ b/solution.py
@@ -11,7 +11,7 @@
 EARLY_ROWS = 128
 LATE_ROWS = 32
 PIECE = 4096
-AHEAD = 4
+AHEAD = 8
 BURST = 16
 SLOTS = 4
 NT = 256

time: 407 us -> 392 us (0.963)
  Pallas kernels: 402 us -> 388 us
    pallas_call x1, Pallas kernels: 402 us -> 388 us  [local(): pl.pallas_call(functools.partial(kernel, n_feat, (W, K, NQ, share, Re, Rl...]
where the time goes in v2:
time: 392 us; the launch traced here: 391 us
  Pallas kernels  388 us (99%)
    pallas_call x1, Pallas kernels, local(): pl.pallas_call(functools.partial(kernel, n_feat, (W, K, NQ, share, Re, Rl...  388 us

profile of v2, /device:TPU:14, one launch (start us, length us, event | category | flops | bytes accessed | tf_op | source)
XLA Modules:
  0.0 390.8 jit_solution(9563276145192519803)
XLA Ops:
  0.0 387.6 %shard_map.37 = (f32[512,1024]{1,0:T(8,128)}, bf16[3,512,16384]{2,1,0:T(8,128)(2,1)}) custom-call(bf16[1024,16384]{1,0:T(8,128)(2,1)} %queries.1, bf16[512,16384]{1,0:T(8,128)(2,1)} %store.1, f32[1,16384]{1,0:T(1,128)} %bitcast.1), custom_call_target="tpu_custom_call" | custom-call | flops 68719476736 | bytes 150994944 | tf_op jit(solution)/shard_map/pallas_call | solution.py:287
  387.6 3.2 copy.5
